TPU v7x, 32 devices: a whole 2x2x4 slice. The times are simulated.
32 devices in a mesh: groups: 2 (over y), row: 4 (over z), col: 4 (over x, core).
Axes of the slice: x: 2, y: 2, z: 4, core: 2. Of those that a mesh axis runs over, the one named last changes fastest.
Arguments:
- view_a: bfloat16 [4096, 8192], P(('groups', 'col'), 'row'), parts along dimension 0, may hold values from -100 to 100
- view_b: bfloat16 [4096, 8192], P(('groups', 'row'), 'col'), parts along dimension 0, may hold values from -100 to 100
Outputs:
- grad_a: float32 [4096, 8192], P(('groups', 'col'), 'row'), parts along dimension 0
- grad_b: float32 [4096, 8192], P(('groups', 'row'), 'col'), parts along dimension 0
There are 2 independent parts, one for each index of `groups`. A program takes and returns all parts, laid end to end along the dimension named above; each array names one. Nothing has to cross between parts.
All inputs are finite; a program needn't handle non-finite values.
Results may differ from a plain program's by a relative error of at most 0.0069.
Values may be sent and summed in bfloat16 or wider, within the bound.
A program may use at most 192 MiB of HBM per device.

v0:
```python
import jax
import jax.numpy as jnp
from jax import lax
from jax.sharding import PartitionSpec as P

EPSILON = 1e-05
OFF_WEIGHT = 0.0051


def standardize(full_view):
    values = full_view.astype(jnp.float32)
    images = values.shape[0]
    column_mean = jnp.sum(values, axis=0) / images
    centered = values - column_mean
    variance = jnp.sum(centered * centered, axis=0) / images
    scale = lax.rsqrt(variance + EPSILON)
    unit_full = centered * scale
    return (unit_full, unit_full.astype(jnp.bfloat16), scale)


def per_device(view_a, view_b):
    rows_a, width_a = view_a.shape
    rows_b, width_b = view_b.shape
    col_count = lax.axis_size("col")
    row_index = lax.axis_index("row")
    col_index = lax.axis_index("col")
    full_a = lax.all_gather(view_a, "col", axis=0, tiled=True)
    full_b = lax.all_gather(view_b, "row", axis=0, tiled=True)
    images = full_a.shape[0]
    unit_a, norm_a, scale_a = standardize(full_a)
    unit_b, norm_b, scale_b = standardize(full_b)
    correlation = (
        lax.dot_general(
            norm_a, norm_b, (((0,), (0,)), ((), ())), preferred_element_type=jnp.float32
        )
        / images
    )
    row_ids = row_index * width_a + jnp.arange(width_a)
    col_ids = col_index * width_b + jnp.arange(width_b)
    on_diagonal = row_ids[:, None] == col_ids[None, :]
    grad_corr = jnp.where(
        on_diagonal, 2.0 * (correlation - 1.0), 2.0 * OFF_WEIGHT * correlation
    ).astype(jnp.bfloat16)
    slab = norm_b
    back_a = lax.psum_scatter(
        lax.dot_general(
            slab, grad_corr, (((1,), (1,)), ((), ())), preferred_element_type=jnp.float32
        ),
        "col",
        scatter_dimension=0,
        tiled=True,
    )
    own_a = lax.dynamic_slice_in_dim(unit_a, col_index * rows_a, rows_a, 0)
    sums_a = jnp.stack([jnp.sum(back_a, axis=0), jnp.sum(back_a * own_a, axis=0)])
    slab = norm_a
    back_b = lax.psum_scatter(
        jnp.dot(slab, grad_corr, preferred_element_type=jnp.float32),
        "row",
        scatter_dimension=0,
        tiled=True,
    )
    own_b = lax.dynamic_slice_in_dim(unit_b, row_index * rows_b, rows_b, 0)
    sums_b = jnp.stack([jnp.sum(back_b, axis=0), jnp.sum(back_b * own_b, axis=0)])
    whole_width = width_b * col_count
    placed_b = lax.dynamic_update_slice(
        jnp.zeros((2, whole_width), jnp.float32), sums_b, (0, col_index * width_b)
    )
    placed_a = lax.dynamic_update_slice(
        jnp.zeros((2, whole_width), jnp.float32), sums_a, (0, row_index * width_a)
    )
    stacked = jnp.concatenate([placed_a, placed_b], axis=0)
    totals = lax.psum(stacked, ("row", "col"))
    total_b = lax.dynamic_slice_in_dim(totals[-2:], col_index * width_b, width_b, 1)
    total_a = lax.dynamic_slice_in_dim(totals[0:2], row_index * width_a, width_a, 1)
    grad_a = scale_a * (back_a - total_a[0] / images - own_a * (total_a[1] / images))
    grad_b = scale_b * (back_b - total_b[0] / images - own_b * (total_b[1] / images))
    return (grad_a, grad_b)


def solution(mesh):
    return jax.shard_map(
        per_device,
        mesh=mesh,
        in_specs=(P(("groups", "col"), "row"), P(("groups", "row"), "col")),
        out_specs=(P(("groups", "col"), "row"), P(("groups", "row"), "col")),
        check_vma=False,
    )
```

profile of v0, /device:TPU:29, one launch (start us, length us, event | category | flops | bytes accessed | tf_op | source)
XLA Modules:
  0.0 795.8 jit_solution(543076985413429680)
XLA Ops:
  7.2 0.7 all-gather.5.cloned.1.call-update
  7.9 0.7 all-gather.3.cloned.1.call-update
  8.7 148.9 %all-gather.5.cloned.1.call-done = bf16[2048,2048]{1,0:T(8,128)(2,1)} async-done(((bf16[512,2048]{1,0:T(8,128)(2,1)}), bf16[2048,2048]{1,0:T(8,128)(2,1)}) %all-gather.5.cloned.1.call-update) | async-done | bytes 8388624 | tf_op jit(solution)/shard_map/all_gather | solution.py:28
  157.6 4.9 convert_reduce_fusion
  162.5 0.8 copy-done
  163.4 2.2 fusion.4
  165.6 53.1 %all-gather.3.cloned.1.call-done = bf16[2048,2048]{1,0:T(8,128)(2,1)} async-done(((bf16[512,2048]{1,0:T(8,128)(2,1)}), bf16[2048,2048]{1,0:T(8,128)(2,1)}) %all-gather.3.cloned.1.call-update) | async-done | bytes 8388624 | tf_op jit(solution)/shard_map/all_gather | solution.py:27
  218.7 4.9 convert_reduce_fusion.1
  223.6 6.4 fusion.5
  230.1 23.0 %select_convert_fusion = bf16[2048,2048]{1,0:T(8,128)(2,1)} fusion(s32[2048]{0:T(1024)S(1)} %get-tuple-element.12, s32[2048]{0:T(1024)S(1)} %get-tuple-element.13, bf16[2048,2048]{1,0:T(8,128)(2,1)S(1)} %copy-done.1, f32[2048]{0:T(1024)S(1)} %add_rsqrt_fusion.1, f32[2048]{0:T(1024)S(1)} %broadcast_multiply_fusion.1, bf16[2048,2048]{1,0:T(8,128)(2,1)S(1)} %bitcast.11, ...), kind=kOutput, calls=%fused_computation.10 | convolution fusion | flops 17242783744 | bytes 25214976 | tf_op jit(solution)/shard_map/dot_general | solution.py:33
  253.1 22.3 %fusion.14 = f32[2048,2048]{1,0:T(8,128)} fusion(bf16[2048,2048]{1,0:T(8,128)(2,1)} %select_convert_fusion, bf16[2048,2048]{1,0:T(8,128)(2,1)S(1)} %bitcast.11, f32[2048]{0:T(1024)S(1)} %add_rsqrt_fusion, f32[2048]{0:T(1024)S(1)} %broadcast_multiply_fusion), kind=kOutput, calls=%fused_computation.19 | convolution fusion | flops 17196646400 | bytes 33570816 | tf_op jit(solution)/shard_map/dot_general | solution.py:46
  275.5 24.6 %fusion.6 = f32[2048,2048]{1,0:T(8,128)} fusion(bf16[2048,2048]{1,0:T(8,128)(2,1)} %select_convert_fusion, bf16[2048,2048]{1,0:T(8,128)(2,1)} %all-gather.3.cloned.1.call-done, f32[2048]{0:T(1024)S(1)} %add_rsqrt_fusion.1, f32[2048]{0:T(1024)S(1)} %broadcast_multiply_fusion.1), kind=kOutput, calls=%fused_computation.15 | convolution fusion | flops 17196646400 | bytes 33570816 | tf_op jit(solution)/shard_map/dot_general | solution.py:57
  300.1 12.3 %fusion = f32[2048,2048]{1,0:T(8,128)} fusion(bf16[2048,2048]{1,0:T(8,128)(2,1)} %all-gather.3.cloned.1.call-done, f32[2048]{0:T(1024)S(1)} %add_rsqrt_fusion.1, f32[2048]{0:T(1024)S(1)} %broadcast_multiply_fusion.1), kind=kLoop, calls=%fused_computation.4 | loop fusion | flops 12582912 | bytes 25182208 | tf_op jit(solution)/shard_map/mul | solution.py:17
  312.5 11.7 %fusion.2 = f32[2048,2048]{1,0:T(8,128)} fusion(bf16[2048,2048]{1,0:T(8,128)(2,1)} %all-gather.5.cloned.1.call-done, f32[2048]{0:T(1024)S(1)} %add_rsqrt_fusion, f32[2048]{0:T(1024)S(1)} %broadcast_multiply_fusion), kind=kLoop, calls=%fused_computation.6 | loop fusion | flops 12582912 | bytes 25182208 | tf_op jit(solution)/shard_map/mul | solution.py:17
  324.1 77.1 %reduce-scatter.3.cloned.1.call-done = f32[512,2048]{1,0:T(8,128)} async-done(((f32[2048,2048]{1,0:T(8,128)}), f32[512,2048]{1,0:T(8,128)}) %reduce-scatter.3.cloned.1.call-update) | async-done | bytes 4194320 | tf_op jit(solution)/shard_map/reduce_scatter | solution.py:45
  401.3 4.5 fusion.19
  405.8 277.9 %reduce-scatter.5.cloned.1.call-done = f32[512,2048]{1,0:T(8,128)} async-done(((f32[2048,2048]{1,0:T(8,128)}), f32[512,2048]{1,0:T(8,128)}) %reduce-scatter.5.cloned.1.call-update) | async-done | bytes 4194320 | tf_op jit(solution)/shard_map/reduce_scatter | solution.py:56
  683.7 4.5 fusion.20
  688.3 0.7 pad_maximum_fusion
  689.0 86.8 %all-reduce.2.cloned.1.call-done = f32[4,8192]{1,0:T(4,128)} async-done(((f32[4,8192]{1,0:T(4,128)}), f32[4,8192]{1,0:T(4,128)}) %all-reduce.2.cloned.1.call-update) | async-done | bytes 131088 | tf_op jit(solution)/shard_map/psum | solution.py:72
  775.8 1.2 fusion.21
  777.0 0.1 dynamic-slice_multiply_fusion.1
  777.2 6.9 subtract_multiply_fusion.1
  784.0 5.2 subtract_multiply_fusion
  (28 shorter events, 0.5 us)
Async XLA Ops:
  7.2 150.4 %all-gather.5.cloned.1.call-start = ((), (), s32[]{:S(2)}) async-start(), calls=%async_computation.3 | async-start | bytes 10485760 | tf_op jit(solution)/shard_map/all_gather | solution.py:28
  7.9 210.8 %all-gather.3.cloned.1.call-start = ((), (), s32[]{:S(2)}) async-start(), calls=%async_computation.2 | async-start | bytes 10485760 | tf_op jit(solution)/shard_map/all_gather | solution.py:27
  8.6 392.6 %reduce-scatter.3.cloned.1.call-start = ((), (), s32[]{:S(2)}) async-start(), calls=%async_computation.4 | async-start | bytes 20971520 | tf_op jit(solution)/shard_map/reduce_scatter | solution.py:45
  157.6 5.8 copy-start
  218.7 11.4 %slice-start = ((s8[8388608]{0:T(1024)(128)(4,1)}), s8[4194304]{0:T(1024)(128)(4,1)S(1)}, s32[]{:S(2)}) async-start(s8[8388608]{0:T(1024)(128)(4,1)} %bitcast.10), calls=%async_computation.7 | async-start | bytes 8388608
  218.7 11.4 %copy-start.1 = (bf16[2048,2048]{1,0:T(8,128)(2,1)S(1)}, bf16[2048,2048]{1,0:T(8,128)(2,1)}, u32[]{:S(2)}) copy-start(bf16[2048,2048]{1,0:T(8,128)(2,1)} %all-gather.3.cloned.1.call-done) | copy-start | bytes 25165828
  223.6 6.5 slice-start.1
  275.4 408.3 %reduce-scatter.5.cloned.1.call-start = ((), (), s32[]{:S(2)}) async-start(), calls=%async_computation.5 | async-start | bytes 20971520 | tf_op jit(solution)/shard_map/reduce_scatter | solution.py:56
  300.1 475.7 %all-reduce.2.cloned.1.call-start = ((), (), s32[]{:S(2)}) async-start(), calls=%async_computation.6 | async-start | bytes 262144 | tf_op jit(solution)/shard_map/psum | solution.py:72
  775.8 8.2 %copy-start.2 = (f32[512,2048]{1,0:T(8,128)S(1)}, f32[512,2048]{1,0:T(8,128)}, u32[]{:S(2)}) copy-start(f32[512,2048]{1,0:T(8,128)} %reduce-scatter.5.cloned.1.call-done) | copy-start | bytes 12582916
Sparse Core Ops, SparseCore 0:
  9.6 147.9 all-gather.4
  159.1 59.5 all-gather.2
  275.5 125.6 reduce-scatter.2
  403.6 280.0 reduce-scatter.4
  689.2 86.5 all-reduce.1
where the time goes:
time: 800 us; the launch traced here: 796 us
  waiting for transfers between devices  645 us (81%)
  matrix products  69.9 us (9%)
  other arithmetic  64.5 us (8%)
  between operations  13.9 us (2%)
    reduce_scatter x1, waiting for transfers between devices, per_device(): lax.psum_scatter(jnp.dot(slab, grad_corr, preferred_element_type=jnp.floa...  278 us
    all_gather x1, waiting for transfers between devices, per_device(): full_b = lax.all_gather(view_b, 'row', axis=0, tiled=True)  149 us
    psum x1, waiting for transfers between devices, per_device(): totals = lax.psum(stacked, ('row', 'col'))  86.8 us
    reduce_scatter x1, waiting for transfers between devices, per_device(): lax.psum_scatter(lax.dot_general(slab, grad_corr, (((1,), (1,)), ((), ())...  77.1 us
    all_gather x1, waiting for transfers between devices, per_device(): full_a = lax.all_gather(view_a, 'col', axis=0, tiled=True)  53.1 us
    dot_general x1, matrix products, per_device(): jnp.dot(slab, grad_corr, preferred_element_type=jnp.float32)  24.6 us
    mul x2, other arithmetic, standardize(): unit_full = centered * scale  24 us
    dot_general x1, matrix products, per_device(): lax.dot_general(norm_a, norm_b, (((0,), (0,)), ((), ())), preferred_eleme...  23 us
  transfers between devices with their start and end apart: 5, of which 5 were waited for; matrix products, arithmetic and copies ran while one was open for 8% of the time, Pallas kernels for 0%

commit v1 on v0

--- a/solution.py
+++ b/solution.py
@@ -18,7 +18,7 @@
     return (unit_full, unit_full.astype(jnp.bfloat16), scale)
 
 
-def per_device(view_a, view_b):
+def per_device_corr(view_a, view_b):
     rows_a, width_a = view_a.shape
     rows_b, width_b = view_b.shape
     col_count = lax.axis_size("col")
@@ -77,7 +77,60 @@
     return (grad_a, grad_b)
 
 
+def per_device_gram(view_a, view_b):
+    rows, _ = view_a.shape
+    side = lax.axis_size("col")
+    col_index = lax.axis_index("col")
+    swap = [(r * side + c, c * side + r) for r in range(side) for c in range(side)]
+    view_b = lax.ppermute(view_b, ("row", "col"), swap)
+    full_a = lax.all_gather(view_a, "col", axis=0, tiled=True)
+    full_b = lax.all_gather(view_b, "col", axis=0, tiled=True)
+    images = full_a.shape[0]
+    unit_a, norm_a, scale_a = standardize(full_a)
+    unit_b, norm_b, scale_b = standardize(full_b)
+    own = lambda x: lax.dynamic_slice_in_dim(x, col_index * rows, rows, 0)
+
+    def gram(norm):
+        part = lax.dot_general(
+            own(norm), norm, (((1,), (1,)), ((), ())), preferred_element_type=jnp.float32
+        )
+        return lax.psum(part.astype(jnp.bfloat16), "row")
+
+    gram_a, gram_b = gram(norm_a), gram(norm_b)
+    diagonal = (
+        jnp.sum(norm_a.astype(jnp.float32) * norm_b.astype(jnp.float32), axis=0) / images
+    )
+    weight = 2.0 * OFF_WEIGHT
+    direct = (2.0 * (diagonal - 1.0)).astype(jnp.bfloat16).astype(jnp.float32)
+    direct = direct - weight * diagonal
+
+    def back(gram_other, norm, other):
+        mixed = jnp.dot(gram_other, norm, preferred_element_type=jnp.float32)
+        return (weight / images) * mixed + direct * own(other).astype(jnp.float32)
+
+    own_a, own_b = own(unit_a), own(unit_b)
+    back_b = back(gram_a, norm_b, norm_a)
+    back_a = back(gram_b, norm_a, norm_b)
+    sums = lax.psum(
+        jnp.stack(
+            [
+                jnp.sum(back_a, axis=0),
+                jnp.sum(back_a * own_a, axis=0),
+                jnp.sum(back_b, axis=0),
+                jnp.sum(back_b * own_b, axis=0),
+            ]
+        ),
+        "col",
+    ) / images
+    grad_b = scale_b * (back_b - sums[2] - own_b * sums[3])
+    grad_b = lax.ppermute(grad_b.astype(jnp.bfloat16), ("row", "col"), swap)
+    grad_a = scale_a * (back_a - sums[0] - own_a * sums[1])
+    return (grad_a, grad_b.astype(jnp.float32))
+
+
 def solution(mesh):
+    square = mesh.shape["row"] == mesh.shape["col"]
+    per_device = per_device_gram if square else per_device_corr
     return jax.shard_map(
         per_device,
         mesh=mesh,

time: 800 us -> 514 us (0.64)
  waiting for transfers between devices: 645 us -> 391 us
  matrix products: 69.9 us -> 39.6 us
  other arithmetic: 64.5 us -> 48.5 us
  blocking collectives: 0 us -> 10.2 us
    reduce_scatter x2 -> x0, waiting for transfers between devices: 355 us -> none  [the longest x1 278 us: per_device(): lax.psum_scatter(jnp.dot(slab, grad_corr, preferred_element_type=jnp.floa...]
    ppermute x0 -> x2, waiting for transfers between devices: none -> 180 us  [the longest x1 92.9 us: per_device_gram(): view_b = lax.ppermute(view_b, ('row', 'col'), swap)]
    all_gather x2, waiting for transfers between devices: 202 us -> 57.7 us  [the longest x1 52.4 us: per_device_gram(): full_b = lax.all_gather(view_b, 'col', axis=0, tiled=True)]
    psum x1, waiting for transfers between devices: 86.8 us -> 153 us  [gram(): return lax.psum(part.astype(jnp.bfloat16), 'row')]
    mul x4 -> x1, other arithmetic: 36.1 us -> 5.21 us  [per_device_gram(): grad_a = scale_a * (back_a - sums[0] - own_a * sums[1])]
    dot_general x3 -> x4, matrix products: 69.9 us -> 39.6 us  [the longest x2 23.8 us: back(): mixed = jnp.dot(gram_other, norm, preferred_element_type=jnp.float32)]
    psum x0 -> x1, blocking collectives: none -> 10.2 us  [per_device_gram(): lax.psum(jnp.stack([jnp.sum(back_a, axis=0), jnp.sum(back_a * own_a, axis...]
    reduce_sum x2 -> x1, other arithmetic: 8.98 us -> 17.5 us  [per_device_gram(): jnp.sum(norm_a.astype(jnp.float32) * norm_b.astype(jnp.float32), axis=0)]
  transfers between devices with their start and end apart: 5 -> 5, of which waited for: 5 -> 5; matrix products, arithmetic and copies ran while one was open for 8% -> 2% of each run, Pallas kernels for 0% -> 0%
where the time goes in v1:
time: 514 us; the launch traced here: 512 us
  waiting for transfers between devices  391 us (76%)
  other arithmetic  48.5 us (9%)
  matrix products  39.6 us (8%)
  between operations  13.9 us (3%)
  blocking collectives  10.2 us (2%)
  starting transfers between devices  6.38 us (1%)
    psum x1, waiting for transfers between devices, gram(): return lax.psum(part.astype(jnp.bfloat16), 'row')  153 us
    ppermute x1, waiting for transfers between devices, per_device_gram(): view_b = lax.ppermute(view_b, ('row', 'col'), swap)  92.9 us
    ppermute x1, waiting for transfers between devices, per_device_gram(): grad_b = lax.ppermute(grad_b.astype(jnp.bfloat16), ('row', 'col'), swap)  86.8 us
    all_gather x1, waiting for transfers between devices, per_device_gram(): full_b = lax.all_gather(view_b, 'col', axis=0, tiled=True)  52.4 us
    dot_general x2, matrix products, back(): mixed = jnp.dot(gram_other, norm, preferred_element_type=jnp.float32)  23.8 us
    reduce_sum x1, other arithmetic, per_device_gram(): jnp.sum(norm_a.astype(jnp.float32) * norm_b.astype(jnp.float32), axis=0)  17.5 us
    dot_general x2, matrix products, gram(): lax.dot_general(own(norm), norm, (((1,), (1,)), ((), ())), preferred_elem...  15.8 us
  transfers between devices with their start and end apart: 5, of which 5 were waited for; matrix products, arithmetic and copies ran while one was open for 2% of the time, Pallas kernels for 0%

profile of v1, /device:TPU:29, one launch (start us, length us, event | category | flops | bytes accessed | tf_op | source)
XLA Modules:
  0.0 512.1 jit_solution(13171358469584715084)
XLA Ops:
  7.2 0.7 all-gather.3.cloned.1.call-update
  7.9 2.9 collective-permute-start
  10.8 92.9 %collective-permute-done = bf16[512,2048]{1,0:T(8,128)(2,1)S(1)} collective-permute-done((bf16[512,2048]{1,0:T(8,128)(2,1)}, bf16[512,2048]{1,0:T(8,128)(2,1)S(1)}, u32[]{:S(2)}, u32[]{:S(2)}) %collective-permute-start) | collective-permute-done | bytes 2097184 | tf_op jit(solution)/shard_map/ppermute | solution.py:85
  103.7 1.3 copy-done.4
  105.1 0.0 all-reduce.3.cloned.1.call-start
  105.1 5.3 %all-gather.3.cloned.1.call-done = bf16[2048,2048]{1,0:T(8,128)(2,1)} async-done(((bf16[512,2048]{1,0:T(8,128)(2,1)}), bf16[2048,2048]{1,0:T(8,128)(2,1)}) %all-gather.3.cloned.1.call-update) | async-done | bytes 8388624 | tf_op jit(solution)/shard_map/all_gather | solution.py:86
  110.4 4.9 convert_reduce_fusion.1
  115.3 0.8 copy-done
  116.2 2.2 fusion.5
  118.4 52.4 %all-gather.5.cloned.1.call-done = bf16[2048,2048]{1,0:T(8,128)(2,1)} async-done(((bf16[512,2048]{1,0:T(8,128)(2,1)}), bf16[2048,2048]{1,0:T(8,128)(2,1)}) %all-gather.5.cloned.1.call-update) | async-done | bytes 8388624 | tf_op jit(solution)/shard_map/all_gather | solution.py:87
  170.9 4.9 convert_reduce_fusion
  175.8 6.4 %fusion.4 = f32[2048]{0:T(1024)S(1)} fusion(bf16[2048,2048]{1,0:T(8,128)(2,1)} %all-gather.5.cloned.1.call-done, f32[2048]{0:T(1024)S(1)} %broadcast_multiply_fusion.1), kind=kLoop, calls=%fused_computation.8 | loop fusion | flops 16775168 | bytes 8404992 | tf_op jit(solution)/shard_map/reduce_sum | solution.py:15
  182.3 17.5 %multiply_reduce_fusion = (f32[2048]{0:T(1024)S(1)}, bf16[2048,2048]{1,0:T(8,128)(2,1)}, bf16[2048,2048]{1,0:T(8,128)(2,1)}, f32[2048,2048]{1,0:T(8,128)}, f32[2048,2048]{1,0:T(8,128)}) fusion(f32[2048]{0:T(1024)S(1)} %add_rsqrt_fusion.1, f32[2048]{0:T(1024)S(1)} %broadcast_multiply_fusion.2, bf16[2048,2048]{1,0:T(8,128)(2,1)S(1)} %bitcast.15, ...), kind=kLoop, calls=%fused_computation.10 | loop fusion | flops 50329600 | bytes 67149824 | tf_op jit(solution)/shard_map/reduce_sum | solution.py:101
  199.7 10.0 %convolution_convert_fusion = bf16[512,2048]{1,0:T(8,128)(2,1)} fusion(bf16[2048,2048]{1,0:T(8,128)(2,1)} %get-tuple-element.9, s32[]{:T(128)S(6)} %select_n.2), kind=kOutput, calls=%fused_computation.17 | convolution fusion | flops 4296015872 | bytes 12582916 | tf_op jit(solution)/shard_map/dot_general | solution.py:94
  209.8 5.7 %convolution_convert_fusion.1 = bf16[512,2048]{1,0:T(8,128)(2,1)} fusion(bf16[2048,2048]{1,0:T(8,128)(2,1)S(1)} %copy-done.2, s32[]{:T(128)S(6)} %select_n.2), kind=kOutput, calls=%fused_computation.18 | convolution fusion | flops 4296015872 | bytes 12582916 | tf_op jit(solution)/shard_map/dot_general | solution.py:94
  215.5 153.3 %all-reduce.3.cloned.1.call-done = (bf16[512,2048]{1,0:T(8,128)(2,1)}, bf16[512,2048]{1,0:T(8,128)(2,1)}) async-done(((bf16[512,2048]{1,0:T(8,128)(2,1)}, bf16[512,2048]{1,0:T(8,128)(2,1)}), (bf16[512,2048]{1,0:T(8,128)(2,1)}, bf16[512,2048]{1,0:T(8,128)(2,1)})) %all-reduce.3.cloned.1.call-update) | async-done | bytes 4194320 | tf_op jit(solution)/shard_map/psum | solution.py:97
  368.8 12.8 %fusion.13 = (f32[2048]{0:T(1024)S(1)}, f32[2048]{0:T(1024)S(1)}, f32[512,2048]{1,0:T(8,128)}) fusion(f32[2048,2048]{1,0:T(8,128)} %get-tuple-element.11, s32[]{:T(128)S(6)} %select_n.2, bf16[2048,2048]{1,0:T(8,128)(2,1)} %get-tuple-element.9, f32[2048]{0:T(1024)S(1)} %multiply_subtract_fusion, bf16[512,2048]{1,0:T(8,128)(2,1)} %get-tuple-element.7, ...), kind=kOutput, calls=%fused_computation.34 | convolution fusion | flops 4302303232 | bytes 20996100 | tf_op jit(solution)/shard_map/dot_general | solution.py:108
  381.6 11.0 %fusion.12 = (f32[2048]{0:T(1024)S(1)}, f32[2048]{0:T(1024)S(1)}, f32[512,2048]{1,0:T(8,128)}) fusion(f32[2048,2048]{1,0:T(8,128)} %get-tuple-element.12, s32[]{:T(128)S(6)} %select_n.2, bf16[2048,2048]{1,0:T(8,128)(2,1)} %get-tuple-element.10, f32[2048]{0:T(1024)S(1)} %multiply_subtract_fusion, bf16[512,2048]{1,0:T(8,128)(2,1)S(1)} %copy-done.5, ...), kind=kOutput, calls=%fused_computation.33 | convolution fusion | flops 4302303232 | bytes 20996100 | tf_op jit(solution)/shard_map/dot_general | solution.py:108
  392.7 10.2 %psum.23 = f32[4,2048]{1,0:T(4,128)S(1)} all-reduce(f32[4,2048]{1,0:T(4,128)S(1)} %pad_maximum_fusion), channel_id=1, replica_groups=mesh['groups'=2,'row'=4,'col'=4] {'col'}, use_global_device_ids=true, to_apply=%region_11.0 | all-reduce | flops 8192 | bytes 65536 | tf_op jit(solution)/shard_map/psum | solution.py:114
  403.0 4.7 multiply_convert_fusion
  407.7 3.4 collective-permute-start.1
  411.1 5.2 %subtract_multiply_fusion = f32[512,2048]{1,0:T(8,128)} fusion(f32[512,2048]{1,0:T(8,128)S(1)} %copy-done.3, f32[2048,2048]{1,0:T(8,128)} %get-tuple-element.12, s32[]{:T(128)S(6)} %select_n.2, f32[2048]{0:T(1024)S(1)} %bitcast.18, f32[2048]{0:T(1024)S(1)} %bitcast.19, f32[2048]{0:T(1024)S(1)} %add_rsqrt_fusion.1), kind=kLoop, calls=%fused_computation.12 | loop fusion | flops 4194304 | bytes 12607492 | tf_op jit(solution)/shard_map/mul | solution.py:127
  416.3 86.8 %collective-permute-done.1 = bf16[512,2048]{1,0:T(8,128)(2,1)S(1)} collective-permute-done((bf16[512,2048]{1,0:T(8,128)(2,1)S(1)}, bf16[512,2048]{1,0:T(8,128)(2,1)S(1)}, u32[]{:S(2)}, u32[]{:S(2)}) %collective-permute-start.1) | collective-permute-done | bytes 2097184 | tf_op jit(solution)/shard_map/ppermute | solution.py:126
  503.0 2.6 convert_element_type.63
  (27 shorter events, 0.2 us)
Async XLA Ops:
  7.2 103.2 %all-gather.3.cloned.1.call-start = ((), (), s32[]{:S(2)}) async-start(), calls=%async_computation | async-start | bytes 10485760 | tf_op jit(solution)/shard_map/all_gather | solution.py:86
  7.9 163.0 %all-gather.5.cloned.1.call-start = ((), (), s32[]{:S(2)}) async-start(), calls=%async_computation.1 | async-start | bytes 10485760 | tf_op jit(solution)/shard_map/all_gather | solution.py:87
  7.9 95.8 %collective-permute-start = (bf16[512,2048]{1,0:T(8,128)(2,1)}, bf16[512,2048]{1,0:T(8,128)(2,1)S(1)}, u32[]{:S(2)}, u32[]{:S(2)}) collective-permute-start(bf16[512,2048]{1,0:T(8,128)(2,1)} %param.3), channel_id=1, source_target_pairs={{0,0},{1,4},{2,8},{3,12},{4,1},{5,5},{6,9},{7,13},{8,2},{9,6},{10,... | collective-permute-start | bytes 6291464 | tf_op jit(solution)/shard_map/ppermute | solution.py:85
  103.7 1.3 copy-start.4
  105.1 263.7 %all-reduce.3.cloned.1.call-start = ((), (), s32[]{:S(2)}) async-start(), calls=%async_computation.2 | async-start | bytes 8388608 | tf_op jit(solution)/shard_map/psum | solution.py:97
  110.4 5.8 %copy-start = (bf16[2048,2048]{1,0:T(8,128)(2,1)S(1)}, bf16[2048,2048]{1,0:T(8,128)(2,1)}, u32[]{:S(2)}) copy-start(bf16[2048,2048]{1,0:T(8,128)(2,1)} %all-gather.3.cloned.1.call-done) | copy-start | bytes 25165828
  170.9 11.4 %slice-start = ((s8[8388608]{0:T(1024)(128)(4,1)}), s8[4194304]{0:T(1024)(128)(4,1)S(1)}, s32[]{:S(2)}) async-start(s8[8388608]{0:T(1024)(128)(4,1)} %bitcast.14), calls=%async_computation.3 | async-start | bytes 8388608
  170.9 11.4 %copy-start.1 = (bf16[2048,2048]{1,0:T(8,128)(2,1)S(1)}, bf16[2048,2048]{1,0:T(8,128)(2,1)}, u32[]{:S(2)}) copy-start(bf16[2048,2048]{1,0:T(8,128)(2,1)} %all-gather.5.cloned.1.call-done) | copy-start | bytes 25165828
  175.8 6.5 %slice-start.1 = ((s8[8388608]{0:T(1024)(128)(4,1)}), s8[4194304]{0:T(1024)(128)(4,1)S(1)}, s32[]{:S(2)}) async-start(s8[8388608]{0:T(1024)(128)(4,1)} %bitcast.14), calls=%async_computation.4 | async-start | bytes 8388608
  199.7 10.0 %copy-start.2 = (bf16[2048,2048]{1,0:T(8,128)(2,1)S(1)}, bf16[2048,2048]{1,0:T(8,128)(2,1)}, u32[]{:S(2)}) copy-start(bf16[2048,2048]{1,0:T(8,128)(2,1)} %get-tuple-element.10) | copy-start | bytes 25165828
  368.8 12.8 %copy-start.5 = (bf16[512,2048]{1,0:T(8,128)(2,1)S(1)}, bf16[512,2048]{1,0:T(8,128)(2,1)}, u32[]{:S(2)}) copy-start(bf16[512,2048]{1,0:T(8,128)(2,1)} %get-tuple-element.6) | copy-start | bytes 6291460
  403.0 8.1 %copy-start.3 = (f32[512,2048]{1,0:T(8,128)S(1)}, f32[512,2048]{1,0:T(8,128)}, u32[]{:S(2)}) copy-start(f32[512,2048]{1,0:T(8,128)} %get-tuple-element.18) | copy-start | bytes 12582916
  407.7 95.4 %collective-permute-start.1 = (bf16[512,2048]{1,0:T(8,128)(2,1)S(1)}, bf16[512,2048]{1,0:T(8,128)(2,1)S(1)}, u32[]{:S(2)}, u32[]{:S(2)}) collective-permute-start(bf16[512,2048]{1,0:T(8,128)(2,1)S(1)} %multiply_convert_fusion), channel_id=1, source_target_pairs={{0,0},{1,4},{2,8},{3,12},{4,1},{5,5},{6,9},{7,13},{8,2},{9,6},{10,... | collective-permute-start | bytes 6291464 | tf_op jit(solution)/shard_map/ppermute | solution.py:126
Sparse Core Ops, SparseCore 0:
  9.6 100.8 all-gather.2
  112.5 58.2 all-gather.4
  215.7 153.1 all-reduce.2

commit v2 on v0

--- a/solution.py
+++ b/solution.py
@@ -1,6 +1,10 @@
+import functools
+
 import jax
 import jax.numpy as jnp
 from jax import lax
+from jax.experimental import pallas as pl
+from jax.experimental.pallas import tpu as pltpu
 from jax.sharding import PartitionSpec as P
 
 EPSILON = 1e-05
@@ -18,7 +22,7 @@
     return (unit_full, unit_full.astype(jnp.bfloat16), scale)
 
 
-def per_device(view_a, view_b):
+def per_device_corr(view_a, view_b):
     rows_a, width_a = view_a.shape
     rows_b, width_b = view_b.shape
     col_count = lax.axis_size("col")
@@ -77,7 +81,434 @@
     return (grad_a, grad_b)
 
 
+MESH = pl.DeviceIdType.MESH
+SIDE = 4
+TILE = 256
+
+
+def gram_kernel(
+    images,
+    na,
+    nb,
+    xa,
+    xb,
+    stats,
+    ga,
+    gb,
+    part,
+    landed,
+    gram,
+    next_row,
+    cross,
+    band,
+    direct,
+    sums,
+    sums_in,
+    grad_send,
+    half_in,
+    relay,
+    final,
+    rs_send,
+    rs_recv,
+    ag_send,
+    ag_recv,
+    plane_send,
+    plane_recv,
+    sum_send,
+    sum_recv,
+    out_send,
+    out_recv,
+    local_sem,
+):
+    g = lax.axis_index("groups")
+    r = lax.axis_index("row")
+    c = lax.axis_index("col")
+    rows, width = xa.shape
+    half = rows // 2
+    chunk = part.shape[1] // SIDE
+    x = c // 2
+    lo = c % 2
+    flip = (c + 2) % SIDE
+    meet = 2 * x + r % 2
+    weight = 2.0 * OFF_WEIGHT
+    norms, raws, backs = (na, nb), (xa, xb), (ga, gb)
+
+    def near(d):
+        return (g, r, (c + d) % SIDE)
+
+    def far(d):
+        return (g, (r + d) % SIDE, c)
+
+    def copy(src, dst, send, recv, to):
+        return pltpu.make_async_remote_copy(
+            src_ref=src,
+            dst_ref=dst,
+            send_sem=send,
+            recv_sem=recv,
+            device_id=to,
+            device_id_type=MESH,
+        )
+
+    barrier = pltpu.get_barrier_semaphore()
+    for d in range(1, SIDE):
+        pl.semaphore_signal(barrier, inc=1, device_id=near(d), device_id_type=MESH)
+        pl.semaphore_signal(barrier, inc=1, device_id=far(d), device_id_type=MESH)
+    odd = (r + c) % 2 == 1
+
+    @pl.when(odd)
+    def _():
+        for plane in (c, flip):
+            pl.semaphore_signal(
+                barrier, inc=1, device_id=(g, plane, meet), device_id_type=MESH
+            )
+        pl.semaphore_wait(barrier, 2 * SIDE)
+
+    @pl.when(jnp.logical_not(odd))
+    def _():
+        pl.semaphore_wait(barrier, 2 * (SIDE - 1))
+
+    def chunk_at(owner):
+        return pl.ds(pl.multiple_of(owner * chunk, 16), chunk)
+
+    def make_part(v):
+        norm = norms[v]
+
+        def body(i, carry):
+            left = jnp.where(i < 4, c * rows + (i % 2) * half, lo * rows + x * half)
+            right = jnp.where(i < 2, c, jnp.where(i < 4, (c + 1) % SIDE, lo + 2)) * rows
+            a = norm[pl.ds(pl.multiple_of(left, half), half), :]
+            b = norm[pl.ds(pl.multiple_of(right, rows), rows), :]
+            t = lax.dot_general(
+                a, b, (((1,), (1,)), ((), ())), preferred_element_type=jnp.float32
+            )
+            part[v, pl.ds(pl.multiple_of(i * half, half), half), :] = t.astype(jnp.bfloat16)
+            return carry
+
+        lax.fori_loop(0, 5, body, 0)
+
+    def rs_copy(v, d):
+        owner = (r + d) % SIDE
+        return copy(
+            part.at[v, chunk_at(owner), :],
+            landed.at[v, d - 1],
+            rs_send.at[v, d - 1],
+            rs_recv.at[v, d - 1],
+            far(d),
+        )
+
+    def ag_copy(v, d):
+        return copy(
+            gram.at[v, chunk_at(r), :],
+            gram.at[v, chunk_at(r), :],
+            ag_send.at[v, d - 1],
+            ag_recv.at[v, d - 1],
+            far(d),
+        )
+
+    def ag_arrival(v, d):
+        owner = (r + SIDE - d) % SIDE
+        return copy(
+            gram.at[v, chunk_at(owner), :],
+            gram.at[v, chunk_at(owner), :],
+            ag_send.at[v, d - 1],
+            ag_recv.at[v, d - 1],
+            far(d),
+        )
+
+    def reduce(v):
+        for d in range(1, SIDE):
+            rs_copy(v, d).wait_recv()
+        total = part[v, chunk_at(r), :].astype(jnp.float32)
+        for d in range(1, SIDE):
+            total = total + landed[v, d - 1].astype(jnp.float32)
+        gram[v, chunk_at(r), :] = total.astype(jnp.bfloat16)
+        for d in range(1, SIDE):
+            ag_copy(v, d).start()
+
+    def plane_copies(v):
+        return (
+            copy(
+                gram.at[v, pl.ds(rows, rows), :],
+                next_row.at[v],
+                plane_send.at[v, 0],
+                plane_recv.at[v, 0],
+                near(1),
+            ),
+            copy(
+                gram.at[v, pl.ds(2 * rows, half), :],
+                cross.at[v],
+                plane_send.at[v, 1],
+                plane_recv.at[v, 1],
+                near(2),
+            ),
+        )
+
+    def share(v):
+        for d in range(1, SIDE):
+            ag_arrival(v, d).wait_recv()
+        for one in plane_copies(v):
+            one.start()
+
+    def turned(block):
+        return block.astype(jnp.float32).T.astype(jnp.bfloat16)
+
+    def make_band(v):
+        for one in plane_copies(v):
+            one.wait_recv()
+        band[c] = gram[v, pl.ds(0, rows), :]
+        band[(c + 1) % SIDE] = gram[v, pl.ds(rows, rows), :]
+        band[(c + 3) % SIDE] = turned(next_row[v])
+
+        @pl.when(x == 0)
+        def _():
+            band[flip, pl.ds(0, half), :] = gram[v, pl.ds(2 * rows, half), :]
+            band[flip, pl.ds(half, half), :] = cross[v]
+
+        @pl.when(x == 1)
+        def _():
+            band[flip, :, pl.ds(0, half)] = turned(cross[v])
+            band[flip, :, pl.ds(half, half)] = turned(gram[v, pl.ds(2 * rows, half), :])
+
+    own = pl.ds(pl.multiple_of(c * rows, rows), rows)
+
+    def unit_of(w, columns):
+        mean = stats[pl.ds(2 * w, 1), columns]
+        scale = stats[pl.ds(2 * w + 1, 1), columns]
+        return (raws[w][:, columns].astype(jnp.float32) - mean) * scale, scale
+
+    def sum_copy(w, d):
+        return copy(
+            sums.at[w],
+            sums_in.at[w, d - 1],
+            sum_send.at[w, d - 1],
+            sum_recv.at[w, d - 1],
+            near(d),
+        )
+
+    def make_back(w):
+        norm, other, back_ref = norms[w], norms[1 - w], backs[w]
+
+        def body(j, carry):
+            columns = pl.ds(pl.multiple_of(j * TILE, TILE), TILE)
+            mixed = jnp.zeros((rows, TILE), jnp.float32)
+            for block in range(SIDE):
+                mixed = mixed + jnp.dot(
+                    band[block],
+                    norm[pl.ds(block * rows, rows), columns],
+                    preferred_element_type=jnp.float32,
+                )
+            term = direct[:, columns] * other[own, columns].astype(jnp.float32)
+            back = (weight / images) * mixed + term
+            unit, _ = unit_of(w, columns)
+            back_ref[:, columns] = back
+            sums[w, pl.ds(0, 1), columns] = jnp.sum(back, axis=0, keepdims=True)
+            sums[w, pl.ds(1, 1), columns] = jnp.sum(back * unit, axis=0, keepdims=True)
+            return carry
+
+        lax.fori_loop(0, width // TILE, body, 0)
+        for d in range(1, SIDE):
+            sum_copy(w, d).start()
+
+    def make_grad(w, target):
+        for d in range(1, SIDE):
+            sum_copy(w, d).wait_recv()
+
+        def body(j, carry):
+            columns = pl.ds(pl.multiple_of(j * TILE, TILE), TILE)
+            total = sums[w, pl.ds(0, 2), columns]
+            for d in range(1, SIDE):
+                total = total + sums_in[w, d - 1, pl.ds(0, 2), columns]
+            total = total / images
+            unit, scale = unit_of(w, columns)
+            grad = scale * (backs[w][:, columns] - total[0:1] - unit * total[1:2])
+            target[:, columns] = grad.astype(target.dtype)
+            return carry
+
+        lax.fori_loop(0, width // TILE, body, 0)
+
+    def make_direct():
+        def body(i, acc):
+            lines = pl.ds(pl.multiple_of(i * 16, 16), 16)
+            prod = na[lines, :].astype(jnp.float32) * nb[lines, :].astype(jnp.float32)
+            return acc + prod[0:8] + prod[8:16]
+
+        acc = lax.fori_loop(0, images // 16, body, jnp.zeros((8, width), jnp.float32))
+        diagonal = jnp.sum(acc, axis=0, keepdims=True) / images
+        rounded = (2.0 * (diagonal - 1.0)).astype(jnp.bfloat16).astype(jnp.float32)
+        direct[...] = rounded - weight * diagonal
+
+    sums[...] = jnp.zeros_like(sums)
+    for v in range(2):
+        make_part(v)
+        for d in range(1, SIDE):
+            rs_copy(v, d).start()
+    make_direct()
+    reduce(0)
+    reduce(1)
+    share(0)
+    make_band(0)
+    make_back(1)
+    make_grad(1, grad_send)
+
+    mine = pl.ds(pl.multiple_of(x * half, half), half)
+    theirs = pl.ds(pl.multiple_of((1 - x) * half, half), half)
+    swap = copy(
+        grad_send.at[theirs, :], half_in, out_send.at[0], out_recv.at[0], near(2)
+    )
+    swap.start()
+    straight = r // 2 == x
+
+    def hop(src, plane, send):
+        @pl.when(straight)
+        def _():
+            copy(
+                src, final.at[mine, :], out_send.at[send], out_recv.at[1], (g, plane, meet)
+            ).start()
+
+        @pl.when(jnp.logical_not(straight))
+        def _():
+            copy(src, relay, out_send.at[send], out_recv.at[2], (g, plane, meet)).start()
+
+    @pl.when(c != r)
+    def _():
+        hop(grad_send.at[mine, :], c, 1)
+
+    @pl.when(c == r)
+    def _():
+        stay = pltpu.make_async_copy(grad_send.at[mine, :], final.at[mine, :], local_sem)
+        stay.start()
+        stay.wait()
+
+    swap.wait_recv()
+
+    @pl.when(flip != r)
+    def _():
+        hop(half_in, flip, 2)
+
+    @pl.when(flip == r)
+    def _():
+        stay = pltpu.make_async_copy(half_in, relay, local_sem)
+        stay.start()
+        stay.wait()
+
+    share(1)
+    make_band(1)
+    make_back(0)
+    make_grad(0, ga)
+
+    forward = copy(relay, final.at[mine, :], out_send.at[3], out_recv.at[3], near(2))
+
+    @pl.when(flip != r)
+    def _():
+        copy(half_in, relay, out_send.at[2], out_recv.at[2], near(2)).wait_recv()
+
+    forward.start()
+
+    @pl.when(c != r)
+    def _():
+        copy(
+            half_in, final.at[mine, :], out_send.at[1], out_recv.at[1], near(2)
+        ).wait_recv()
+
+    copy(relay, final.at[theirs, :], out_send.at[3], out_recv.at[3], near(2)).wait_recv()
+
+    def widen(i, carry):
+        lines = pl.ds(pl.multiple_of(i * 16, 16), 16)
+        gb[lines, :] = final[lines, :].astype(jnp.float32)
+        return carry
+
+    lax.fori_loop(0, rows // 16, widen, 0)
+
+    for v in range(2):
+        for d in range(1, SIDE):
+            rs_copy(v, d).wait_send()
+            ag_copy(v, d).wait_send()
+            sum_copy(v, d).wait_send()
+        for one in plane_copies(v):
+            one.wait_send()
+    swap.wait_send()
+    forward.wait_send()
+
+    @pl.when(c != r)
+    def _():
+        copy(
+            grad_send.at[mine, :], relay, out_send.at[1], out_recv.at[1], near(2)
+        ).wait_send()
+
+    @pl.when(flip != r)
+    def _():
+        copy(half_in, relay, out_send.at[2], out_recv.at[2], near(2)).wait_send()
+
+
+def gram_gradients(norm_a, norm_b, own_a, own_b, stats):
+    images, width = norm_a.shape
+    rows = images // SIDE
+    half = rows // 2
+    whole = pl.BlockSpec(memory_space=pltpu.VMEM)
+    out = jax.ShapeDtypeStruct((rows, width), jnp.float32)
+    bf16, f32 = jnp.bfloat16, jnp.float32
+    dma = pltpu.SemaphoreType.DMA
+    return pl.pallas_call(
+        functools.partial(gram_kernel, images),
+        out_shape=(out, out),
+        in_specs=[whole] * 5,
+        out_specs=(whole, whole),
+        scratch_shapes=[
+            pltpu.VMEM((2, 2 * rows + half, rows), bf16),
+            pltpu.VMEM((2, SIDE - 1, (2 * rows + half) // SIDE, rows), bf16),
+            pltpu.VMEM((2, 2 * rows + half, rows), bf16),
+            pltpu.VMEM((2, rows, rows), bf16),
+            pltpu.VMEM((2, half, rows), bf16),
+            pltpu.VMEM((SIDE, rows, rows), bf16),
+            pltpu.VMEM((1, width), f32),
+            pltpu.VMEM((2, 8, width), f32),
+            pltpu.VMEM((2, SIDE - 1, 8, width), f32),
+            pltpu.VMEM((rows, width), bf16),
+            pltpu.VMEM((half, width), bf16),
+            pltpu.VMEM((half, width), bf16),
+            pltpu.VMEM((rows, width), bf16),
+            dma((2, SIDE - 1)),
+            dma((2, SIDE - 1)),
+            dma((2, SIDE - 1)),
+            dma((2, SIDE - 1)),
+            dma((2, 2)),
+            dma((2, 2)),
+            dma((2, SIDE - 1)),
+            dma((2, SIDE - 1)),
+            dma((4,)),
+            dma((4,)),
+            dma,
+        ],
+        compiler_params=pltpu.CompilerParams(
+            collective_id=0, has_side_effects=True, vmem_limit_bytes=60 * 2**20
+        ),
+    )(norm_a, norm_b, own_a, own_b, stats)
+
+
+def standardize_parts(full_view):
+    values = full_view.astype(jnp.float32)
+    images = values.shape[0]
+    column_mean = jnp.sum(values, axis=0) / images
+    centered = values - column_mean
+    scale = lax.rsqrt(jnp.sum(centered * centered, axis=0) / images + EPSILON)
+    return ((centered * scale).astype(jnp.bfloat16), column_mean, scale)
+
+
+def per_device_gram(view_a, view_b):
+    swap = [(r * SIDE + c, c * SIDE + r) for r in range(SIDE) for c in range(SIDE)]
+    view_b = lax.ppermute(view_b, ("row", "col"), swap)
+    full_a = lax.all_gather(view_a, "col", axis=0, tiled=True)
+    full_b = lax.all_gather(view_b, "col", axis=0, tiled=True)
+    norm_a, mean_a, scale_a = standardize_parts(full_a)
+    norm_b, mean_b, scale_b = standardize_parts(full_b)
+    zero = jnp.zeros_like(mean_a)
+    stats = jnp.stack([mean_a, scale_a, mean_b, scale_b, zero, zero, zero, zero])
+    return gram_gradients(norm_a, norm_b, view_a, view_b, stats)
+
+
 def solution(mesh):
+    square = mesh.shape["row"] == SIDE and mesh.shape["col"] == SIDE
+    per_device = per_device_gram if square else per_device_corr
     return jax.shard_map(
         per_device,
         mesh=mesh,

time: 800 us -> 418 us (0.52)
  waiting for transfers between devices: 645 us -> 140 us
  Pallas kernels: 0 us -> 212 us
  matrix products: 69.9 us -> 0 us
  other arithmetic: 64.5 us -> 35.2 us
  local copies, waits for them, and re-layouts: 2.06 us -> 10.6 us
    reduce_scatter x2 -> x0, waiting for transfers between devices: 355 us -> none  [the longest x1 278 us: per_device(): lax.psum_scatter(jnp.dot(slab, grad_corr, preferred_element_type=jnp.floa...]
    pallas_call x0 -> x1, Pallas kernels: none -> 212 us  [gram_gradients(): pl.pallas_call(functools.partial(gram_kernel, images), out_shape=(out, ou...]
    all_gather x2, waiting for transfers between devices: 202 us -> 46.8 us  [the longest x1 41.5 us: per_device_gram(): full_b = lax.all_gather(view_b, 'col', axis=0, tiled=True)]
    ppermute x0 -> x1, waiting for transfers between devices: none -> 92.9 us  [per_device_gram(): view_b = lax.ppermute(view_b, ('row', 'col'), swap)]
    psum x1 -> x0, waiting for transfers between devices: 86.8 us -> none  [per_device(): totals = lax.psum(stacked, ('row', 'col'))]
    dot_general x3 -> x0, matrix products: 69.9 us -> none  [the longest x1 24.6 us: per_device(): jnp.dot(slab, grad_corr, preferred_element_type=jnp.float32)]
    mul x4 -> x0, other arithmetic: 36.1 us -> none  [the longest x2 24 us: standardize(): unit_full = centered * scale]
    convert_element_type x0 -> x2, other arithmetic: none -> 20.9 us  [standardize_parts(): return ((centered * scale).astype(jnp.bfloat16), column_mean, scale)]
  transfers between devices with their start and end apart: 5 -> 3, of which waited for: 5 -> 3; matrix products, arithmetic and copies ran while one was open for 8% -> 4% of each run, Pallas kernels for 0% -> 0%
where the time goes in v2:
time: 418 us; the launch traced here: 416 us
  Pallas kernels  212 us (51%)
  waiting for transfers between devices  140 us (33%)
  other arithmetic  35.2 us (8%)
  between operations  14.1 us (3%)
  local copies, waits for them, and re-layouts  10.6 us (3%)
    pallas_call x1, Pallas kernels, gram_gradients(): pl.pallas_call(functools.partial(gram_kernel, images), out_shape=(out, ou...  212 us
    ppermute x1, waiting for transfers between devices, per_device_gram(): view_b = lax.ppermute(view_b, ('row', 'col'), swap)  92.9 us
    all_gather x1, waiting for transfers between devices, per_device_gram(): full_b = lax.all_gather(view_b, 'col', axis=0, tiled=True)  41.5 us
    convert_element_type x2, other arithmetic, standardize_parts(): return ((centered * scale).astype(jnp.bfloat16), column_mean, scale)  20.9 us
    unnamed x10, local copies, waits for them, and re-layouts  9.86 us
    reduce_sum x2, other arithmetic, standardize_parts(): column_mean = jnp.sum(values, axis=0) / images  9.84 us
  transfers between devices with their start and end apart: 3, of which 3 were waited for; matrix products, arithmetic and copies ran while one was open for 4% of the time, Pallas kernels for 0%

profile of v2, /device:TPU:29, one launch (start us, length us, event | category | flops | bytes accessed | tf_op | source)
XLA Modules:
  0.0 415.6 jit_solution(7281206063051856553)
XLA Ops:
  7.2 0.0 all-gather.3.cloned.1.call-start
  7.2 0.7 all-gather.3.cloned.1.call-update
  7.9 0.0 all-gather.5.cloned.1.call-start
  7.9 2.9 collective-permute-start
  10.8 92.9 %collective-permute-done.xb = bf16[512,2048]{1,0:T(8,128)(2,1)S(1)} collective-permute-done((bf16[512,2048]{1,0:T(8,128)(2,1)}, bf16[512,2048]{1,0:T(8,128)(2,1)S(1)}, u32[]{:S(2)}, u32[]{:S(2)}) %collective-permute-start) | collective-permute-done | bytes 2097184 | tf_op jit(solution)/shard_map/ppermute | solution.py:499
  103.7 0.0 copy-start.2
  103.7 1.3 copy-done.2
  105.1 0.0 all-gather.5.cloned.1.call-update
  105.1 5.3 %all-gather.3.cloned.1.call-done = bf16[2048,2048]{1,0:T(8,128)(2,1)} async-done(((bf16[512,2048]{1,0:T(8,128)(2,1)}), bf16[2048,2048]{1,0:T(8,128)(2,1)}) %all-gather.3.cloned.1.call-update) | async-done | bytes 8388624 | tf_op jit(solution)/shard_map/all_gather | solution.py:500
  110.4 4.9 %convert_reduce_fusion.1 = f32[2048]{0:T(1024)S(1)} fusion(bf16[2048,2048]{1,0:T(8,128)(2,1)} %all-gather.3.cloned.1.call-done), kind=kLoop, calls=%fused_computation.3 | loop fusion | flops 8386560 | bytes 8396800 | tf_op jit(solution)/shard_map/reduce_sum | solution.py:491
  115.3 0.8 copy-done
  116.2 2.2 fusion.6
  118.4 10.9 %fusion.7.na = bf16[2048,2048]{1,0:T(8,128)(2,1)} fusion(bf16[2048,2048]{1,0:T(8,128)(2,1)} %all-gather.3.cloned.1.call-done, f32[2048]{0:T(1024)S(1)} %add_rsqrt_fusion.1, f32[2048]{0:T(1024)S(1)} %broadcast_multiply_fusion.1), kind=kLoop, calls=%fused_computation.11 | loop fusion | flops 16777216 | bytes 16793600 | tf_op jit(solution)/shard_map/convert_element_type | solution.py:494
  129.4 41.5 %all-gather.5.cloned.1.call-done = bf16[2048,2048]{1,0:T(8,128)(2,1)} async-done(((bf16[512,2048]{1,0:T(8,128)(2,1)}), bf16[2048,2048]{1,0:T(8,128)(2,1)}) %all-gather.5.cloned.1.call-update) | async-done | bytes 8388624 | tf_op jit(solution)/shard_map/all_gather | solution.py:501
  170.9 4.9 %convert_reduce_fusion = f32[2048]{0:T(1024)S(1)} fusion(bf16[2048,2048]{1,0:T(8,128)(2,1)} %all-gather.5.cloned.1.call-done), kind=kLoop, calls=%fused_computation.1 | loop fusion | flops 8386560 | bytes 8396800 | tf_op jit(solution)/shard_map/reduce_sum | solution.py:491
  175.8 0.8 copy-done.1
  176.6 2.2 fusion.4
  178.9 0.7 stack.5.stats
  179.6 10.0 %fusion.5.nb = bf16[2048,2048]{1,0:T(8,128)(2,1)} fusion(bf16[2048,2048]{1,0:T(8,128)(2,1)} %all-gather.5.cloned.1.call-done, f32[2048]{0:T(1024)S(1)} %add_rsqrt_fusion, f32[2048]{0:T(1024)S(1)} %broadcast_multiply_fusion), kind=kLoop, calls=%fused_computation.9 | loop fusion | flops 16777216 | bytes 16793600 | tf_op jit(solution)/shard_map/convert_element_type | solution.py:494
  189.5 212.3 %shard_map.41 = (f32[512,2048]{1,0:T(8,128)}, f32[512,2048]{1,0:T(8,128)}) custom-call(bf16[2048,2048]{1,0:T(8,128)(2,1)} %fusion.7.na, bf16[2048,2048]{1,0:T(8,128)(2,1)} %fusion.5.nb, bf16[512,2048]{1,0:T(8,128)(2,1)} %xa.1, bf16[512,2048]{1,0:T(8,128)(2,1)} %copy-done.2, f32[8,2048]{1,0:T(8,128)} %stack.5.stats), custom_call_target="tpu_custom_call" | custom-call | tf_op jit(solution)/shard_map/pallas_call | solution.py:451
  401.8 0.0 copy-start.3
  401.8 4.8 %copy.6 = f32[512,2048]{1,0:T(8,128)} copy(f32[512,2048]{1,0:T(8,128)} %get-tuple-element.4) | data formatting | bytes 8388608
  406.7 0.0 copy-done.3
  406.7 2.0 copy.7
  (7 shorter events, 0.0 us)
Async XLA Ops:
  7.2 103.2 %all-gather.3.cloned.1.call-start = ((), (), s32[]{:S(2)}) async-start(), calls=%async_computation | async-start | bytes 10485760 | tf_op jit(solution)/shard_map/all_gather | solution.py:500
  7.9 163.0 %all-gather.5.cloned.1.call-start = ((), (), s32[]{:S(2)}) async-start(), calls=%async_computation.1 | async-start | bytes 10485760 | tf_op jit(solution)/shard_map/all_gather | solution.py:501
  7.9 95.8 %collective-permute-start = (bf16[512,2048]{1,0:T(8,128)(2,1)}, bf16[512,2048]{1,0:T(8,128)(2,1)S(1)}, u32[]{:S(2)}, u32[]{:S(2)}) collective-permute-start(bf16[512,2048]{1,0:T(8,128)(2,1)} %param.3), channel_id=1, source_target_pairs={{0,0},{1,4},{2,8},{3,12},{4,1},{5,5},{6,9},{7,13},{8,2},{9,6},{10,... | collective-permute-start | bytes 6291464 | tf_op jit(solution)/shard_map/ppermute | solution.py:499
  103.7 1.3 copy-start.2
  110.4 5.8 %copy-start = (bf16[2048,2048]{1,0:T(8,128)(2,1)S(1)}, bf16[2048,2048]{1,0:T(8,128)(2,1)}, u32[]{:S(2)}) copy-start(bf16[2048,2048]{1,0:T(8,128)(2,1)} %all-gather.3.cloned.1.call-done) | copy-start | bytes 25165828
  170.9 5.8 %copy-start.1 = (bf16[2048,2048]{1,0:T(8,128)(2,1)S(1)}, bf16[2048,2048]{1,0:T(8,128)(2,1)}, u32[]{:S(2)}) copy-start(bf16[2048,2048]{1,0:T(8,128)(2,1)} %all-gather.5.cloned.1.call-done) | copy-start | bytes 25165828
  401.8 4.9 %copy-start.3 = (f32[512,2048]{1,0:T(8,128)S(1)}, f32[512,2048]{1,0:T(8,128)}, u32[]{:S(2)}) copy-start(f32[512,2048]{1,0:T(8,128)} %get-tuple-element.5) | copy-start | bytes 12582916
Sparse Core Ops, SparseCore 0:
  9.6 100.8 all-gather.2
  112.5 58.2 all-gather.4

commit v3 on v2

--- a/solution.py
+++ b/solution.py
@@ -88,13 +88,15 @@
 
 def gram_kernel(
     images,
+    xa,
+    raw_b,
+    ga,
+    gb,
     na,
     nb,
-    xa,
     xb,
     stats,
-    ga,
-    gb,
+    half_b,
     part,
     landed,
     gram,
@@ -118,7 +120,14 @@
     sum_recv,
     out_send,
     out_recv,
+    a_send,
+    a_recv,
+    b_send,
+    b_recv,
+    bg_send,
+    bg_recv,
     local_sem,
+    own_sem,
 ):
     g = lax.axis_index("groups")
     r = lax.axis_index("row")
@@ -131,6 +140,11 @@
     flip = (c + 2) % SIDE
     meet = 2 * x + r % 2
     weight = 2.0 * OFF_WEIGHT
+    own = pl.ds(pl.multiple_of(c * rows, rows), rows)
+    mine = pl.ds(pl.multiple_of(x * half, half), half)
+    theirs = pl.ds(pl.multiple_of((1 - x) * half, half), half)
+    straight = r // 2 == x
+    sibling = (g, r, c + 1 - 2 * lo)
     norms, raws, backs = (na, nb), (xa, xb), (ga, gb)
 
     def near(d):
@@ -269,8 +283,6 @@
             band[flip, :, pl.ds(0, half)] = turned(cross[v])
             band[flip, :, pl.ds(half, half)] = turned(gram[v, pl.ds(2 * rows, half), :])
 
-    own = pl.ds(pl.multiple_of(c * rows, rows), rows)
-
     def unit_of(w, columns):
         mean = stats[pl.ds(2 * w, 1), columns]
         scale = stats[pl.ds(2 * w + 1, 1), columns]
@@ -337,26 +349,174 @@
         rounded = (2.0 * (diagonal - 1.0)).astype(jnp.bfloat16).astype(jnp.float32)
         direct[...] = rounded - weight * diagonal
 
+    def block_of(b):
+        return pl.ds(pl.multiple_of(b * rows, rows), rows)
+
+    def half_of(b, h):
+        return pl.ds(pl.multiple_of(b * rows + h * half, half), half)
+
+    def lines_of(i):
+        return pl.ds(pl.multiple_of(i * 32, 32), 32)
+
+    def fold(values):
+        return values[0:8] + values[8:16] + values[16:24] + values[24:32]
+
+    def standardize_in_place(w):
+        norm = norms[w]
+        zero = jnp.zeros((8, width), jnp.float32)
+
+        def add(i, acc):
+            return acc + fold(norm[lines_of(i), :].astype(jnp.float32))
+
+        acc = lax.fori_loop(0, images // 32, add, zero)
+        mean = jnp.sum(acc, axis=0, keepdims=True) / images
+        stats[pl.ds(2 * w, 1), :] = mean
+
+        def add_square(i, acc):
+            centered = norm[lines_of(i), :].astype(jnp.float32) - stats[pl.ds(2 * w, 1), :]
+            return acc + fold(centered * centered)
+
+        acc = lax.fori_loop(0, images // 32, add_square, zero)
+        variance = jnp.sum(acc, axis=0, keepdims=True) / images
+        stats[pl.ds(2 * w + 1, 1), :] = lax.rsqrt(variance + EPSILON)
+
+        def write(i, carry):
+            centered = norm[lines_of(i), :].astype(jnp.float32) - stats[pl.ds(2 * w, 1), :]
+            unit = centered * stats[pl.ds(2 * w + 1, 1), :]
+            norm[lines_of(i), :] = unit.astype(jnp.bfloat16)
+            return carry
+
+        lax.fori_loop(0, images // 32, write, 0)
+
     sums[...] = jnp.zeros_like(sums)
-    for v in range(2):
-        make_part(v)
-        for d in range(1, SIDE):
-            rs_copy(v, d).start()
+
+    a_side = copy(xa, na.at[own, :], a_send.at[0], a_recv.at[0], sibling)
+    a_cross = copy(xa, na.at[own, :], a_send.at[1], a_recv.at[1], near(2))
+    a_pass = copy(
+        na.at[block_of(flip), :],
+        na.at[block_of(flip), :],
+        a_send.at[2],
+        a_recv.at[2],
+        sibling,
+    )
+    a_own = pltpu.make_async_copy(xa, na.at[own, :], own_sem)
+    b_swap = copy(raw_b.at[theirs, :], half_b, b_send.at[0], b_recv.at[0], near(2))
+    b_place = nb.at[half_of(r, x), :]
+
+    def b_hop(src, plane, send):
+        @pl.when(straight)
+        def _():
+            copy(
+                src, b_place, b_send.at[send], b_recv.at[1], (g, plane, meet)
+            ).start()
+
+        @pl.when(jnp.logical_not(straight))
+        def _():
+            copy(
+                src, b_place, b_send.at[send], b_recv.at[2], (g, plane, meet)
+            ).start()
+
+    b_swap.start()
+    a_side.start()
+    a_own.start()
+
+    @pl.when(c != r)
+    def _():
+        b_hop(raw_b.at[mine, :], c, 1)
+
+    @pl.when(c == r)
+    def _():
+        stay = pltpu.make_async_copy(raw_b.at[mine, :], b_place, local_sem)
+        stay.start()
+        stay.wait()
+
+    b_swap.wait_recv()
+    a_cross.start()
+
+    @pl.when(flip != r)
+    def _():
+        b_hop(half_b, flip, 2)
+
+    @pl.when(flip == r)
+    def _():
+        stay = pltpu.make_async_copy(half_b, b_place, local_sem)
+        stay.start()
+        stay.wait()
+
+    a_cross.wait_recv()
+    a_pass.start()
+
+    def b_spread(k):
+        block = c if k == 0 else flip
+        here = nb.at[half_of(block, x), :]
+        came = nb.at[half_of(flip if k == 0 else c, 1 - x), :]
+        return (
+            copy(here, here, bg_send.at[k, 0], bg_recv.at[k, 0], sibling),
+            copy(here, here, bg_send.at[k, 1], bg_recv.at[k, 1], near(2)),
+            copy(came, came, bg_send.at[k, 2], bg_recv.at[k, 2], sibling),
+        )
+
+    @pl.when(c != r)
+    def _():
+        here = nb.at[half_of(c, x), :]
+        copy(here, here, b_send.at[1], b_recv.at[1], near(2)).wait_recv()
+
+    b_spread(0)[1].start()
+    b_spread(0)[0].start()
+
+    @pl.when(flip != r)
+    def _():
+        here = nb.at[half_of(flip, x), :]
+        copy(here, here, b_send.at[2], b_recv.at[2], near(2)).wait_recv()
+
+    b_spread(1)[1].start()
+    b_spread(1)[0].start()
+
+    other_col = c + 1 - 2 * lo
+    far_col = (other_col + 2) % SIDE
+
+    def arrived(ref, place, recv):
+        copy(ref.at[place, :], ref.at[place, :], a_send.at[0], recv, near(2)).wait_recv()
+
+    a_own.wait()
+    arrived(na, block_of(other_col), a_recv.at[0])
+    arrived(na, block_of(far_col), a_recv.at[2])
+    a_side.wait_send()
+    a_cross.wait_send()
+    a_pass.wait_send()
+    standardize_in_place(0)
+    make_part(0)
+    for d in range(1, SIDE):
+        rs_copy(0, d).start()
+    reduce(0)
+
+    for k in range(2):
+        arrived(nb, half_of(flip if k == 0 else c, 1 - x), bg_recv.at[k, 1])
+        b_spread(k)[2].start()
+    for k in range(2):
+        arrived(nb, half_of(other_col if k == 0 else far_col, x), bg_recv.at[k, 0])
+        arrived(nb, half_of(far_col if k == 0 else other_col, 1 - x), bg_recv.at[k, 2])
+    for k in range(2):
+        for one in b_spread(k):
+            one.wait_send()
+    keep = pltpu.make_async_copy(nb.at[own, :], xb, local_sem)
+    keep.start()
+    keep.wait()
+    standardize_in_place(1)
+    make_part(1)
+    for d in range(1, SIDE):
+        rs_copy(1, d).start()
     make_direct()
-    reduce(0)
-    reduce(1)
     share(0)
     make_band(0)
     make_back(1)
+    reduce(1)
     make_grad(1, grad_send)
 
-    mine = pl.ds(pl.multiple_of(x * half, half), half)
-    theirs = pl.ds(pl.multiple_of((1 - x) * half, half), half)
     swap = copy(
         grad_send.at[theirs, :], half_in, out_send.at[0], out_recv.at[0], near(2)
     )
     swap.start()
-    straight = r // 2 == x
 
     def hop(src, plane, send):
         @pl.when(straight)
@@ -426,6 +586,7 @@
             sum_copy(v, d).wait_send()
         for one in plane_copies(v):
             one.wait_send()
+    b_swap.wait_send()
     swap.wait_send()
     forward.wait_send()
 
@@ -434,15 +595,17 @@
         copy(
             grad_send.at[mine, :], relay, out_send.at[1], out_recv.at[1], near(2)
         ).wait_send()
+        copy(raw_b.at[mine, :], half_b, b_send.at[1], b_recv.at[1], near(2)).wait_send()
 
     @pl.when(flip != r)
     def _():
         copy(half_in, relay, out_send.at[2], out_recv.at[2], near(2)).wait_send()
-
-
-def gram_gradients(norm_a, norm_b, own_a, own_b, stats):
-    images, width = norm_a.shape
-    rows = images // SIDE
+        copy(half_b, half_in, b_send.at[2], b_recv.at[2], near(2)).wait_send()
+
+
+def gram_gradients(view_a, view_b):
+    rows, width = view_a.shape
+    images = SIDE * rows
     half = rows // 2
     whole = pl.BlockSpec(memory_space=pltpu.VMEM)
     out = jax.ShapeDtypeStruct((rows, width), jnp.float32)
@@ -451,9 +614,14 @@
     return pl.pallas_call(
         functools.partial(gram_kernel, images),
         out_shape=(out, out),
-        in_specs=[whole] * 5,
+        in_specs=[whole] * 2,
         out_specs=(whole, whole),
         scratch_shapes=[
+            pltpu.VMEM((images, width), bf16),
+            pltpu.VMEM((images, width), bf16),
+            pltpu.VMEM((rows, width), bf16),
+            pltpu.VMEM((8, width), f32),
+            pltpu.VMEM((half, width), bf16),
             pltpu.VMEM((2, 2 * rows + half, rows), bf16),
             pltpu.VMEM((2, SIDE - 1, (2 * rows + half) // SIDE, rows), bf16),
             pltpu.VMEM((2, 2 * rows + half, rows), bf16),
@@ -477,38 +645,24 @@
             dma((2, SIDE - 1)),
             dma((4,)),
             dma((4,)),
+            dma((3,)),
+            dma((3,)),
+            dma((3,)),
+            dma((3,)),
+            dma((2, 3)),
+            dma((2, 3)),
+            dma,
             dma,
         ],
         compiler_params=pltpu.CompilerParams(
-            collective_id=0, has_side_effects=True, vmem_limit_bytes=60 * 2**20
+            collective_id=1, has_side_effects=True, vmem_limit_bytes=60 * 2**20
         ),
-    )(norm_a, norm_b, own_a, own_b, stats)
-
-
-def standardize_parts(full_view):
-    values = full_view.astype(jnp.float32)
-    images = values.shape[0]
-    column_mean = jnp.sum(values, axis=0) / images
-    centered = values - column_mean
-    scale = lax.rsqrt(jnp.sum(centered * centered, axis=0) / images + EPSILON)
-    return ((centered * scale).astype(jnp.bfloat16), column_mean, scale)
-
-
-def per_device_gram(view_a, view_b):
-    swap = [(r * SIDE + c, c * SIDE + r) for r in range(SIDE) for c in range(SIDE)]
-    view_b = lax.ppermute(view_b, ("row", "col"), swap)
-    full_a = lax.all_gather(view_a, "col", axis=0, tiled=True)
-    full_b = lax.all_gather(view_b, "col", axis=0, tiled=True)
-    norm_a, mean_a, scale_a = standardize_parts(full_a)
-    norm_b, mean_b, scale_b = standardize_parts(full_b)
-    zero = jnp.zeros_like(mean_a)
-    stats = jnp.stack([mean_a, scale_a, mean_b, scale_b, zero, zero, zero, zero])
-    return gram_gradients(norm_a, norm_b, view_a, view_b, stats)
+    )(view_a, view_b)
 
 
 def solution(mesh):
     square = mesh.shape["row"] == SIDE and mesh.shape["col"] == SIDE
-    per_device = per_device_gram if square else per_device_corr
+    per_device = gram_gradients if square else per_device_corr
     return jax.shard_map(
         per_device,
         mesh=mesh,

time: 418 us -> 290 us (0.69)
  waiting for transfers between devices: 140 us -> 0 us
  Pallas kernels: 212 us -> 282 us
  other arithmetic: 35.2 us -> 0 us
  between operations: 14.1 us -> 0.65 us
    ppermute x1 -> x0, waiting for transfers between devices: 92.9 us -> none  [per_device_gram(): view_b = lax.ppermute(view_b, ('row', 'col'), swap)]
    pallas_call x1, Pallas kernels: 212 us -> 282 us  [gram_gradients(): pl.pallas_call(functools.partial(gram_kernel, images), out_shape=(out, ou...]
    all_gather x2 -> x0, waiting for transfers between devices: 46.8 us -> none  [the longest x1 41.5 us: per_device_gram(): full_b = lax.all_gather(view_b, 'col', axis=0, tiled=True)]
    convert_element_type x2 -> x0, other arithmetic: 20.9 us -> none  [standardize_parts(): return ((centered * scale).astype(jnp.bfloat16), column_mean, scale)]
    reduce_sum x4 -> x0, other arithmetic: 14.3 us -> none  [the longest x2 9.84 us: standardize_parts(): column_mean = jnp.sum(values, axis=0) / images]
    unnamed x10 -> x4, local copies, waits for them, and re-layouts: 9.86 us -> 6.87 us
  transfers between devices with their start and end apart: 3 -> 0, of which waited for: 3 -> 0; matrix products, arithmetic and copies ran while one was open for 4% -> 0% of each run, Pallas kernels for 0% -> 0%
where the time goes in v3:
time: 290 us
  Pallas kernels  282 us (97%)
  local copies, waits for them, and re-layouts  6.87 us (2%)
    pallas_call x1, Pallas kernels, gram_gradients(): pl.pallas_call(functools.partial(gram_kernel, images), out_shape=(out, ou...  282 us
    unnamed x4, local copies, waits for them, and re-layouts  6.87 us

profile of v3, /device:TPU:29, one launch (start us, length us, event | category | flops | bytes accessed | tf_op | source)
XLA Modules:
  0.0 289.7 jit_solution(16171229256020555041)
XLA Ops:
  0.6 282.1 %shard_map.41 = (f32[512,2048]{1,0:T(8,128)}, f32[512,2048]{1,0:T(8,128)}) custom-call(bf16[512,2048]{1,0:T(8,128)(2,1)} %xa.1, bf16[512,2048]{1,0:T(8,128)(2,1)} %raw_b.1), custom_call_target="tpu_custom_call" | custom-call | tf_op jit(solution)/shard_map/pallas_call | solution.py:614
  282.8 0.0 copy-start
  282.8 4.8 %copy.6 = f32[512,2048]{1,0:T(8,128)} copy(f32[512,2048]{1,0:T(8,128)} %get-tuple-element.4) | data formatting | bytes 8388608
  287.6 0.0 copy-done
  287.6 2.0 copy.7
Async XLA Ops:
  282.8 4.9 %copy-start = (f32[512,2048]{1,0:T(8,128)S(1)}, f32[512,2048]{1,0:T(8,128)}, u32[]{:S(2)}) copy-start(f32[512,2048]{1,0:T(8,128)} %get-tuple-element.5) | copy-start | bytes 12582916

commit v4 on v3

--- a/solution.py
+++ b/solution.py
@@ -97,6 +97,7 @@
     xb,
     stats,
     half_b,
+    back_b,
     part,
     landed,
     gram,
@@ -145,7 +146,7 @@
     theirs = pl.ds(pl.multiple_of((1 - x) * half, half), half)
     straight = r // 2 == x
     sibling = (g, r, c + 1 - 2 * lo)
-    norms, raws, backs = (na, nb), (xa, xb), (ga, gb)
+    norms, raws, backs = (na, nb), (xa, xb), (ga, back_b)
 
     def near(d):
         return (g, r, (c + d) % SIDE)
@@ -513,25 +514,49 @@
     reduce(1)
     make_grad(1, grad_send)
 
+    quarter = half // 2
+
+    def final_at(h, q):
+        return final.at[
+            pl.ds(pl.multiple_of(h * half + q * quarter, quarter), quarter), :
+        ]
+
+    def mine_at(q):
+        return grad_send.at[
+            pl.ds(pl.multiple_of(x * half + q * quarter, quarter), quarter), :
+        ]
+
+    def relay_at(q):
+        return relay.at[pl.ds(q * quarter, quarter), :]
+
+    def half_in_at(q):
+        return half_in.at[pl.ds(q * quarter, quarter), :]
+
     swap = copy(
-        grad_send.at[theirs, :], half_in, out_send.at[0], out_recv.at[0], near(2)
+        grad_send.at[theirs, :], half_in, out_send.at[0, 0], out_recv.at[0, 0], near(2)
     )
     swap.start()
 
     def hop(src, plane, send):
-        @pl.when(straight)
-        def _():
-            copy(
-                src, final.at[mine, :], out_send.at[send], out_recv.at[1], (g, plane, meet)
-            ).start()
-
-        @pl.when(jnp.logical_not(straight))
-        def _():
-            copy(src, relay, out_send.at[send], out_recv.at[2], (g, plane, meet)).start()
+        to = (g, plane, meet)
+        for q in range(2):
+            piece = src(q)
+
+            @pl.when(straight)
+            def _():
+                copy(
+                    piece, final_at(x, q), out_send.at[send, q], out_recv.at[1, q], to
+                ).start()
+
+            @pl.when(jnp.logical_not(straight))
+            def _():
+                copy(
+                    piece, relay_at(q), out_send.at[send, q], out_recv.at[2, q], to
+                ).start()
 
     @pl.when(c != r)
     def _():
-        hop(grad_send.at[mine, :], c, 1)
+        hop(mine_at, c, 1)
 
     @pl.when(c == r)
     def _():
@@ -543,7 +568,7 @@
 
     @pl.when(flip != r)
     def _():
-        hop(half_in, flip, 2)
+        hop(half_in_at, flip, 2)
 
     @pl.when(flip == r)
     def _():
@@ -554,30 +579,38 @@
     share(1)
     make_band(1)
     make_back(0)
+
+    def forward(q):
+        return copy(
+            relay_at(q), final_at(x, q), out_send.at[3, q], out_recv.at[3, q], near(2)
+        )
+
+    def pass_on(q):
+        @pl.when(flip != r)
+        def _():
+            copy(
+                relay_at(q), relay_at(q), out_send.at[2, q], out_recv.at[2, q], near(2)
+            ).wait_recv()
+
+        forward(q).start()
+
+    pass_on(0)
     make_grad(0, ga)
-
-    forward = copy(relay, final.at[mine, :], out_send.at[3], out_recv.at[3], near(2))
-
-    @pl.when(flip != r)
-    def _():
-        copy(half_in, relay, out_send.at[2], out_recv.at[2], near(2)).wait_recv()
-
-    forward.start()
-
-    @pl.when(c != r)
-    def _():
+    pass_on(1)
+
+    for q in range(2):
+
+        @pl.when(c != r)
+        def _():
+            copy(
+                mine_at(q), final_at(x, q), out_send.at[1, q], out_recv.at[1, q], near(2)
+            ).wait_recv()
+
+    for q in range(2):
         copy(
-            half_in, final.at[mine, :], out_send.at[1], out_recv.at[1], near(2)
+            relay_at(q), final_at(1 - x, q), out_send.at[3, q], out_recv.at[3, q], near(2)
         ).wait_recv()
-
-    copy(relay, final.at[theirs, :], out_send.at[3], out_recv.at[3], near(2)).wait_recv()
-
-    def widen(i, carry):
-        lines = pl.ds(pl.multiple_of(i * 16, 16), 16)
-        gb[lines, :] = final[lines, :].astype(jnp.float32)
-        return carry
-
-    lax.fori_loop(0, rows // 16, widen, 0)
+    gb[...] = final[...]
 
     for v in range(2):
         for d in range(1, SIDE):
@@ -588,18 +621,23 @@
             one.wait_send()
     b_swap.wait_send()
     swap.wait_send()
-    forward.wait_send()
+    forward(0).wait_send()
+    forward(1).wait_send()
 
     @pl.when(c != r)
     def _():
-        copy(
-            grad_send.at[mine, :], relay, out_send.at[1], out_recv.at[1], near(2)
-        ).wait_send()
+        for q in range(2):
+            copy(
+                mine_at(q), relay_at(q), out_send.at[1, q], out_recv.at[1, q], near(2)
+            ).wait_send()
         copy(raw_b.at[mine, :], half_b, b_send.at[1], b_recv.at[1], near(2)).wait_send()
 
     @pl.when(flip != r)
     def _():
-        copy(half_in, relay, out_send.at[2], out_recv.at[2], near(2)).wait_send()
+        for q in range(2):
+            copy(
+                half_in_at(q), relay_at(q), out_send.at[2, q], out_recv.at[2, q], near(2)
+            ).wait_send()
         copy(half_b, half_in, b_send.at[2], b_recv.at[2], near(2)).wait_send()
 
 
@@ -611,9 +649,9 @@
     out = jax.ShapeDtypeStruct((rows, width), jnp.float32)
     bf16, f32 = jnp.bfloat16, jnp.float32
     dma = pltpu.SemaphoreType.DMA
-    return pl.pallas_call(
+    grad_a, grad_b = pl.pallas_call(
         functools.partial(gram_kernel, images),
-        out_shape=(out, out),
+        out_shape=(out, jax.ShapeDtypeStruct((rows, width), jnp.bfloat16)),
         in_specs=[whole] * 2,
         out_specs=(whole, whole),
         scratch_shapes=[
@@ -622,6 +660,7 @@
             pltpu.VMEM((rows, width), bf16),
             pltpu.VMEM((8, width), f32),
             pltpu.VMEM((half, width), bf16),
+            pltpu.VMEM((rows, width), f32),
             pltpu.VMEM((2, 2 * rows + half, rows), bf16),
             pltpu.VMEM((2, SIDE - 1, (2 * rows + half) // SIDE, rows), bf16),
             pltpu.VMEM((2, 2 * rows + half, rows), bf16),
@@ -643,8 +682,8 @@
             dma((2, 2)),
             dma((2, SIDE - 1)),
             dma((2, SIDE - 1)),
-            dma((4,)),
-            dma((4,)),
+            dma((4, 2)),
+            dma((4, 2)),
             dma((3,)),
             dma((3,)),
             dma((3,)),
@@ -658,6 +697,7 @@
             collective_id=1, has_side_effects=True, vmem_limit_bytes=60 * 2**20
         ),
     )(view_a, view_b)
+    return (grad_a, grad_b.astype(jnp.float32))
 
 
 def solution(mesh):

time: 290 us -> 285 us (0.983)
  Pallas kernels: 282 us -> 277 us
  local copies, waits for them, and re-layouts: 6.87 us -> 2.02 us
  other arithmetic: 0 us -> 4.28 us
    unnamed x4 -> x3, local copies, waits for them, and re-layouts: 6.87 us -> 2.02 us
    pallas_call x1, Pallas kernels: 282 us -> 277 us  [gram_gradients(): pl.pallas_call(functools.partial(gram_kernel, images), out_shape=(out, ja...]
    convert_element_type x0 -> x1, other arithmetic: none -> 4.28 us  [gram_gradients(): return (grad_a, grad_b.astype(jnp.float32))]
where the time goes in v4:
time: 285 us; the launch traced here: 284 us
  Pallas kernels  277 us (97%)
  other arithmetic  4.28 us (2%)
    pallas_call x1, Pallas kernels, gram_gradients(): pl.pallas_call(functools.partial(gram_kernel, images), out_shape=(out, ja...  277 us

profile of v4, /device:TPU:29, one launch (start us, length us, event | category | flops | bytes accessed | tf_op | source)
XLA Modules:
  0.0 284.4 jit_solution(5798196834190141733)
XLA Ops:
  0.6 277.4 %shard_map.41 = (f32[512,2048]{1,0:T(8,128)}, bf16[512,2048]{1,0:T(8,128)(2,1)}) custom-call(bf16[512,2048]{1,0:T(8,128)(2,1)} %xa.1, bf16[512,2048]{1,0:T(8,128)(2,1)} %raw_b.1), custom_call_target="tpu_custom_call" | custom-call | tf_op jit(solution)/shard_map/pallas_call | solution.py:652
  278.1 0.0 copy-start
  278.1 4.3 %convert_element_type.3 = f32[512,2048]{1,0:T(8,128)} convert(bf16[512,2048]{1,0:T(8,128)(2,1)} %get-tuple-element.5) | non-fusion elementwise | flops 1048576 | bytes 6291456 | tf_op jit(solution)/shard_map/convert_element_type | solution.py:700
  282.4 0.0 copy-done
  282.4 2.0 copy.5
Async XLA Ops:
  278.1 4.3 %copy-start = (f32[512,2048]{1,0:T(8,128)S(1)}, f32[512,2048]{1,0:T(8,128)}, u32[]{:S(2)}) copy-start(f32[512,2048]{1,0:T(8,128)} %get-tuple-element.8) | copy-start | bytes 12582916

commit v5 on v4

--- a/solution.py
+++ b/solution.py
@@ -417,7 +417,7 @@
                 src, b_place, b_send.at[send], b_recv.at[2], (g, plane, meet)
             ).start()
 
-    b_swap.start()
+    a_cross.start()
     a_side.start()
     a_own.start()
 
@@ -431,20 +431,8 @@
         stay.start()
         stay.wait()
 
-    b_swap.wait_recv()
-    a_cross.start()
-
-    @pl.when(flip != r)
-    def _():
-        b_hop(half_b, flip, 2)
-
-    @pl.when(flip == r)
-    def _():
-        stay = pltpu.make_async_copy(half_b, b_place, local_sem)
-        stay.start()
-        stay.wait()
-
     a_cross.wait_recv()
+    b_swap.start()
     a_pass.start()
 
     def b_spread(k):
@@ -456,22 +444,6 @@
             copy(here, here, bg_send.at[k, 1], bg_recv.at[k, 1], near(2)),
             copy(came, came, bg_send.at[k, 2], bg_recv.at[k, 2], sibling),
         )
-
-    @pl.when(c != r)
-    def _():
-        here = nb.at[half_of(c, x), :]
-        copy(here, here, b_send.at[1], b_recv.at[1], near(2)).wait_recv()
-
-    b_spread(0)[1].start()
-    b_spread(0)[0].start()
-
-    @pl.when(flip != r)
-    def _():
-        here = nb.at[half_of(flip, x), :]
-        copy(here, here, b_send.at[2], b_recv.at[2], near(2)).wait_recv()
-
-    b_spread(1)[1].start()
-    b_spread(1)[0].start()
 
     other_col = c + 1 - 2 * lo
     far_col = (other_col + 2) % SIDE
@@ -489,6 +461,34 @@
     make_part(0)
     for d in range(1, SIDE):
         rs_copy(0, d).start()
+    b_swap.wait_recv()
+
+    @pl.when(flip != r)
+    def _():
+        b_hop(half_b, flip, 2)
+
+    @pl.when(flip == r)
+    def _():
+        stay = pltpu.make_async_copy(half_b, b_place, local_sem)
+        stay.start()
+        stay.wait()
+
+    @pl.when(c != r)
+    def _():
+        here = nb.at[half_of(c, x), :]
+        copy(here, here, b_send.at[1], b_recv.at[1], near(2)).wait_recv()
+
+    b_spread(0)[1].start()
+    b_spread(0)[0].start()
+
+    @pl.when(flip != r)
+    def _():
+        here = nb.at[half_of(flip, x), :]
+        copy(here, here, b_send.at[2], b_recv.at[2], near(2)).wait_recv()
+
+    b_spread(1)[1].start()
+    b_spread(1)[0].start()
+
     reduce(0)
 
     for k in range(2):

time: 285 us -> 334 us (1.17)
  Pallas kernels: 277 us -> 326 us
    pallas_call x1, Pallas kernels: 277 us -> 326 us  [gram_gradients(): pl.pallas_call(functools.partial(gram_kernel, images), out_shape=(out, ja...]
where the time goes in v5:
time: 334 us; the launch traced here: 333 us
  Pallas kernels  326 us (98%)
  other arithmetic  4.28 us (1%)
    pallas_call x1, Pallas kernels, gram_gradients(): pl.pallas_call(functools.partial(gram_kernel, images), out_shape=(out, ja...  326 us

profile of v5, /device:TPU:29, one launch (start us, length us, event | category | flops | bytes accessed | tf_op | source)
XLA Modules:
  0.0 332.6 jit_solution(670879215291810113)
XLA Ops:
  0.6 325.6 %shard_map.41 = (f32[512,2048]{1,0:T(8,128)}, bf16[512,2048]{1,0:T(8,128)(2,1)}) custom-call(bf16[512,2048]{1,0:T(8,128)(2,1)} %xa.1, bf16[512,2048]{1,0:T(8,128)(2,1)} %raw_b.1), custom_call_target="tpu_custom_call" | custom-call | tf_op jit(solution)/shard_map/pallas_call | solution.py:652
  326.3 0.0 copy-start
  326.3 4.3 %convert_element_type.3 = f32[512,2048]{1,0:T(8,128)} convert(bf16[512,2048]{1,0:T(8,128)(2,1)} %get-tuple-element.5) | non-fusion elementwise | flops 1048576 | bytes 6291456 | tf_op jit(solution)/shard_map/convert_element_type | solution.py:700
  330.6 0.0 copy-done
  330.6 2.0 copy.5
Async XLA Ops:
  326.3 4.3 %copy-start = (f32[512,2048]{1,0:T(8,128)S(1)}, f32[512,2048]{1,0:T(8,128)}, u32[]{:S(2)}) copy-start(f32[512,2048]{1,0:T(8,128)} %get-tuple-element.8) | copy-start | bytes 12582916
